TPU v7x, 32 devices: a whole 2x2x4 slice. The times are simulated.
32 devices in a mesh: enc: 4 (over y, x), seq: 2 (over core), exp: 4 (over z).
Axes of the slice: x: 2, y: 2, z: 4, core: 2. Of those that a mesh axis runs over, the one named last changes fastest.
Arguments:
- tokens: bfloat16 [4096, 2048], P(('enc', 'seq', 'exp')), may hold values from -6 to 6
- frames: bfloat16 [2048, 1024], P(('enc', 'seq', 'exp')), may hold values from -6 to 6
- w_patch: bfloat16 [1024, 1280], P(None, 'seq'), may hold values from -0.1875 to 0.1875
- w_proj: bfloat16 [1280, 2048], P('seq'), may hold values from -0.15625 to 0.15625
- clip_len: int32 [128], P(('enc', 'seq', 'exp')), may hold values from 1 to 16, as said below
- clip_start: int32 [128], P(('enc', 'seq', 'exp')), may hold values from 0 to 127, as said below
- expert_ids: int32 [4096, 8], P(('enc', 'seq', 'exp')), may hold values from 0 to 15, all different within a row; in each aligned block of 128 rows (0 to 127, 128 to 255, ...) at most 80 rows name the same one
- gate_score: float32 [4096, 8], P(('enc', 'seq', 'exp')), may hold values from 0.05 to 1
- cotangent: bfloat16 [4096, 2048], P(('enc', 'seq', 'exp')), may hold values from -0.29882812 to 0.29882812
- w_gate: bfloat16 [16, 2048, 768], P(('enc', 'exp')), may hold values from -0.125 to 0.125
- w_up: bfloat16 [16, 2048, 768], P(('enc', 'exp')), may hold values from -0.125 to 0.125
- w_down: bfloat16 [16, 768, 2048], P(('enc', 'exp')), may hold values from -0.21875 to 0.21875
Outputs:
- moe_out: bfloat16 [4096, 2048], P(('enc', 'seq', 'exp'))
- score_grad: float32 [4096, 8], P(('enc', 'seq', 'exp'))
Inputs may be any that keep to these rules, and one draw needn't show every extreme that they name: `clip_len`: every clip has 1 to 16 rows; in every group of devices that share their seq and exp indices some clip has exactly 16 rows. The clip from the encoder device at enc index e lies inside token rows e * 32 to (e + 1) * 32 - 1 of the receiving device: clip_start + clip_len <= (e + 1) * 32, so clips never share a row. `expert_ids`: among the tokens of one device no expert is named more than 80 times, and in every draw some expert is named exactly 80 times by some device's tokens.
All inputs are finite; a program needn't handle non-finite values.
Results may differ from a plain program's by a relative error of at most 0.0085.
Values may be sent and summed in bfloat16 or wider, within the bound.
A program may use at most 128 MiB of HBM per device.

v0:
```python
import jax
import jax.numpy as jnp
from jax import lax
from jax.sharding import PartitionSpec as P


def expert_rows(rows, gate_mat, up_mat, down_mat):
    gate_part = jnp.dot(rows, gate_mat, preferred_element_type=jnp.float32)
    up_part = jnp.dot(rows, up_mat, preferred_element_type=jnp.float32)
    active = (jax.nn.silu(gate_part) * up_part).astype(jnp.bfloat16)
    return jnp.dot(active, down_mat, preferred_element_type=jnp.float32).astype(jnp.bfloat16)


def per_device(
    tokens,
    frames,
    w_patch,
    w_proj,
    clip_len,
    clip_start,
    expert_ids,
    gate_score,
    cotangent,
    w_gate,
    w_up,
    w_down,
):
    audio_count = frames.shape[0]
    width = tokens.shape[1]
    tok_count = tokens.shape[0]
    top_count = expert_ids.shape[1]
    enc_count = lax.axis_size("enc")
    exp_count = lax.axis_size("exp")
    clip_rows = audio_count // enc_count
    grouped = lax.all_gather(frames, "seq", axis=0, tiled=True)
    hidden_cols = jax.nn.gelu(
        jnp.dot(grouped, w_patch, preferred_element_type=jnp.float32), approximate=False
    ).astype(jnp.bfloat16)
    embedded = lax.psum_scatter(
        jnp.dot(hidden_cols, w_proj, preferred_element_type=jnp.float32),
        "seq",
        scatter_dimension=0,
        tiled=True,
    )
    embedded = embedded.astype(jnp.bfloat16).reshape(enc_count, clip_rows, width)
    arrived, lengths, starts = (
        lax.all_to_all(embedded, "enc", split_axis=0, concat_axis=0, tiled=True),
        lax.all_to_all(clip_len, "enc", split_axis=0, concat_axis=0, tiled=True),
        lax.all_to_all(clip_start, "enc", split_axis=0, concat_axis=0, tiled=True),
    )
    offsets = jnp.arange(clip_rows, dtype=jnp.int32)
    positions = jnp.where(
        offsets[None, :] < lengths[:, None], starts[:, None] + offsets[None, :], -1
    ).reshape(-1)
    selector = jnp.arange(tok_count, dtype=jnp.int32)[:, None] == positions[None, :]
    placed = jnp.dot(
        selector.astype(jnp.bfloat16),
        arrived.reshape(-1, width),
        preferred_element_type=jnp.float32,
    )
    mixed = jnp.where(jnp.any(selector, axis=1)[:, None], placed.astype(jnp.bfloat16), tokens)
    experts = enc_count * exp_count
    capacity = tok_count * top_count * 5 // (4 * experts)
    flat_ids = expert_ids.reshape(-1)
    onehot = (flat_ids[:, None] == jnp.arange(experts, dtype=jnp.int32)[None, :]).astype(jnp.int32)
    slots = jnp.sum(jnp.cumsum(onehot, axis=0) * onehot, axis=1) - 1
    targets = flat_ids * capacity + slots
    placing = jnp.arange(experts * capacity, dtype=jnp.int32)[:, None] == targets[None, :]
    placing = jnp.any(placing.reshape(experts * capacity, tok_count, top_count), axis=2)
    outgoing = jnp.dot(
        placing.astype(jnp.bfloat16), mixed, preferred_element_type=jnp.float32
    ).astype(jnp.bfloat16)
    outgoing = outgoing.reshape(experts, capacity, width)
    received = lax.all_to_all(outgoing, ("enc", "exp"), split_axis=0, concat_axis=0, tiled=True)
    sources = received.shape[0]
    items = received.shape[1]
    result = expert_rows(received.reshape(sources * items, width), w_gate[0], w_up[0], w_down[0])
    results = lax.all_to_all(
        result.reshape(sources, items, width),
        ("enc", "exp"),
        split_axis=0,
        concat_axis=0,
        tiled=True,
    )
    results = results.reshape(experts * capacity, width)
    picked = results[targets].reshape(tok_count, top_count, width)
    total = jnp.sum(gate_score, axis=-1, keepdims=True)
    gate = gate_score / total
    moe_out = jnp.einsum("tk,tkd->td", gate, picked.astype(jnp.float32)).astype(jnp.bfloat16)
    score_dot = jnp.einsum("td,tkd->tk", cotangent, picked, preferred_element_type=jnp.float32)
    score_grad = (score_dot - jnp.sum(gate * score_dot, axis=-1, keepdims=True)) / total
    return (moe_out, score_grad)


def solution(mesh):
    in_specs = (
        P(("enc", "seq", "exp"), None),
        P(("enc", "seq", "exp"), None),
        P(None, "seq"),
        P("seq", None),
        P(("enc", "seq", "exp")),
        P(("enc", "seq", "exp")),
        P(("enc", "seq", "exp"), None),
        P(("enc", "seq", "exp"), None),
        P(("enc", "seq", "exp"), None),
        P(("enc", "exp"), None, None),
        P(("enc", "exp"), None, None),
        P(("enc", "exp"), None, None),
    )
    out_specs = (P(("enc", "seq", "exp"), None), P(("enc", "seq", "exp"), None))
    return jax.shard_map(
        per_device, mesh=mesh, in_specs=in_specs, out_specs=out_specs, check_vma=False
    )
```

profile of v0, /device:TPU:0, one launch (start us, length us, event | category | flops | bytes accessed | tf_op | source)
XLA Modules:
  0.0 354.3 jit_solution(9569177147054433289)
XLA Ops:
  7.2 2.4 all_gather.3
  9.7 4.7 %fusion.23 = f32[128,2048]{1,0:T(8,128)} fusion(bf16[640,2048]{1,0:T(8,128)(2,1)} %param.15, bf16[128,1024]{1,0:T(8,128)(2,1)S(1)} %all_gather.3, bf16[1024,640]{1,0:T(8,128)(2,1)} %param.14), kind=kOutput, calls=%fused_computation.39 | convolution fusion | flops 508641280 | bytes 5242880 | tf_op jit(solution)/shard_map/dot_general | solution.py:40
  14.4 0.7 copy.42
  15.1 5.1 %all-to-all-start = ((s32[4,1,1]{2,1,0:T(1,128)}), s32[4,1,1]{2,1,0:T(1,128)S(1)}, u32[]{:S(2)}, u32[]{:S(2)}) async-start(s32[4,1,1]{2,1,0:T(1,128)} %copy.42), calls=%async_computation | async-start | bytes 4096 | tf_op jit(solution)/shard_map/all_to_all | solution.py:48
  20.2 0.1 copy.36
  20.3 0.1 eq.57
  20.5 4.5 %reduce-window.6 = s32[16,8,128]{2,1,0:T(8,128)S(1)} reduce-window(s32[16,8,128]{2,1,0:T(8,128)S(1)} %fusion.57, s32[]{:T(128)} %constant.37.clone.1), window={size=1x1x128 pad=0_0x0_0x127_0}, to_apply=%region_1.2 | reduce-window | flops 2080768 | bytes 131076 | tf_op jit(solution)/shard_map/reduce-window
  25.1 0.1 copy.39
  25.6 0.7 copy.43
  26.3 5.3 %fusion = pred[1280,128]{1,0:T(8,128)(4,1)} fusion(s32[128,8]{0,1:T(8,128)S(1)} %copy.41), kind=kLoop, calls=%fused_computation.4 | loop fusion | flops 2457600 | bytes 167936 | tf_op jit(solution)/shard_map/reduce_or | solution.py:69
  31.6 4.2 %all-to-all-start.1 = ((s32[4,1,1]{2,1,0:T(1,128)}), s32[4,1,1]{2,1,0:T(1,128)S(1)}, u32[]{:S(2)}, u32[]{:S(2)}) async-start(s32[4,1,1]{2,1,0:T(1,128)} %copy.43), calls=%async_computation.1 | async-start | bytes 4096 | tf_op jit(solution)/shard_map/all_to_all | solution.py:49
  35.8 0.2 reduce
  35.9 4.4 %all-to-all-done.1 = s32[4,1,1]{2,1,0:T(1,128)S(1)} async-done(((s32[4,1,1]{2,1,0:T(1,128)}), s32[4,1,1]{2,1,0:T(1,128)S(1)}, u32[]{:S(2)}, u32[]{:S(2)}) %all-to-all-start.1) | async-done | bytes 48 | tf_op jit(solution)/shard_map/all_to_all | solution.py:49
  40.3 0.2 reduce.1
  40.5 1.8 convert_element_type.31
  42.3 3.4 all-to-all-start.2
  45.9 0.1 fusion.58
  46.0 5.1 %all-to-all-done.2 = bf16[4,16,2048]{2,1,0:T(8,128)(2,1)S(1)} async-done(((bf16[4,16,2048]{2,1,0:T(8,128)(2,1)}), bf16[4,16,2048]{2,1,0:T(8,128)(2,1)S(1)}, u32[]{:S(2)}, u32[]{:S(2)}) %all-to-all-start.2) | async-done | bytes 262176 | tf_op jit(solution)/shard_map/all_to_all | solution.py:47
  51.0 5.2 %convolution_convert_fusion.1 = bf16[1280,2048]{1,0:T(8,128)(2,1)} fusion(pred[1280,128]{1,0:T(8,128)(4,1)} %fusion, bf16[128,2048]{1,0:T(8,128)(2,1)} %param.12, bf16[64,2048]{1,0:T(8,128)(2,1)S(1)} %bitcast.64, pred[128]{0:T(512)(128)(4,1)S(1)} %fusion.58, s32[64]{0:T(128)S(1)} %select_n.26), kind=kOutput, calls=%fused_computation.2 | convolution fusion | flops 707796992 | bytes 6193536 | tf_op jit(solution)/shard_map/dot_general | solution.py:70
  56.3 120.7 %all_to_all.33 = bf16[16,80,2048]{2,1,0:T(8,128)(2,1)S(1)} all-to-all(bf16[16,80,2048]{2,1,0:T(8,128)(2,1)} %bitcast.60), channel_id=1, replica_groups=mesh['enc'=4,'seq'=2,'exp'=4] {'enc','exp'}, dimensions={0} | all-to-all | bytes 10485760 | tf_op jit(solution)/shard_map/all_to_all | solution.py:74
  177.0 4.3 %fusion.8 = f32[1280,768]{1,0:T(8,128)S(1)} fusion(bf16[1280,2048]{1,0:T(8,128)(2,1)S(1)} %bitcast.62, bf16[1,2048,768]{2,1,0:T(8,128)(2,1)S(1)} %copy-done.5), kind=kOutput, calls=%fused_computation.13 | convolution fusion | flops 4026531840 | bytes 12320768 | tf_op jit(solution)/shard_map/dot_general | solution.py:8
  181.4 4.8 %fusion.5 = bf16[1280,768]{1,0:T(8,128)(2,1)S(1)} fusion(bf16[1280,2048]{1,0:T(8,128)(2,1)S(1)} %bitcast.63, f32[1280,768]{1,0:T(8,128)S(1)} %fusion.8, bf16[1,2048,768]{2,1,0:T(8,128)(2,1)S(1)} %copy-done.6), kind=kOutput, calls=%fused_computation.10 | convolution fusion | flops 4032430080 | bytes 14286848 | tf_op jit(solution)/shard_map/dot_general | solution.py:9
  186.2 6.0 %convolution_convert_fusion = bf16[1280,2048]{1,0:T(8,128)(2,1)} fusion(bf16[1280,768]{1,0:T(8,128)(2,1)S(1)} %fusion.5, bf16[1,768,2048]{2,1,0:T(8,128)(2,1)S(1)} %copy-done), kind=kOutput, calls=%fused_computation.1 | convolution fusion | flops 4029153280 | bytes 10354688 | tf_op jit(solution)/shard_map/dot_general | solution.py:11
  192.2 4.9 %all-to-all-start.4 = ((bf16[16,80,2048]{2,1,0:T(8,128)(2,1)}), bf16[16,80,2048]{2,1,0:T(8,128)(2,1)}, u32[]{:S(2)}, u32[]{:S(2)}) async-start(bf16[16,80,2048]{2,1,0:T(8,128)(2,1)} %bitcast.61), calls=%async_computation.5 | async-start | bytes 10485760 | tf_op jit(solution)/shard_map/all_to_all | solution.py:78
  197.2 0.1 mul.58
  197.3 0.1 copy.44
  197.5 127.7 %all-to-all-done.4 = bf16[16,80,2048]{2,1,0:T(8,128)(2,1)} async-done(((bf16[16,80,2048]{2,1,0:T(8,128)(2,1)}), bf16[16,80,2048]{2,1,0:T(8,128)(2,1)}, u32[]{:S(2)}, u32[]{:S(2)}) %all-to-all-start.4) | async-done | bytes 5242912 | tf_op jit(solution)/shard_map/all_to_all | solution.py:78
  325.2 12.0 %gather_fusion = bf16[1024,2048]{1,0:T(8,128)(2,1)} fusion(bf16[1280,2048]{1,0:T(8,128)(2,1)} %bitcast.13, s32[1024]{0:T(1024)S(1)} %broadcast_clamp_fusion), kind=kCustom, calls=%fused_computation | custom fusion | bytes 8392704 | tf_op jit(solution)/shard_map/gather | solution.py:86
  337.2 5.0 %fusion.1 = f32[128,1,8]{2,1,0:T(1,128)S(1)} fusion(bf16[1024,2048]{1,0:T(8,128)(2,1)} %gather_fusion, bf16[128,2048,1]{1,0,2:T(8,128)(2,1)} %bitcast.73), kind=kOutput, calls=%fused_computation.5 | convolution fusion | flops 4194304 | bytes 4722688 | tf_op jit(solution)/shard_map/td,tkd->tk/dot_general | solution.py:90
  342.3 0.6 fusion.62
  342.9 3.4 fusion.3
  346.3 1.1 copy.53
  (38 shorter events, 0.9 us)
Async XLA Ops:
  7.2 179.0 %copy-start = (bf16[1,768,2048]{2,1,0:T(8,128)(2,1)S(1)}, bf16[1,768,2048]{2,1,0:T(8,128)(2,1)}, u32[]{:S(2)}) copy-start(bf16[1,768,2048]{2,1,0:T(8,128)(2,1)} %param.23) | copy-start | bytes 9437188
  7.2 33.3 %reduce-scatter.2.cloned.1.call-start = ((), (), s32[]{:S(2)}) async-start(), calls=%async_computation.6 | async-start | bytes 1572864 | tf_op jit(solution)/shard_map/reduce_scatter | solution.py:39
  9.7 4.7 %copy-start.3 = (s32[4]{0:T(128)S(1)}, s32[4]{0:T(128)}, u32[]{:S(2)}) copy-start(s32[4]{0:T(128)} %param.16) | copy-start | bytes 52
  9.7 10.5 %copy-start.2 = (s32[128,8]{0,1:T(8,128)S(1)}, s32[128,8]{0,1:T(8,128)}, u32[]{:S(2)}) copy-start(s32[128,8]{0,1:T(8,128)} %param.18) | copy-start | bytes 12292
  9.7 15.9 %copy-start.4 = (s32[4]{0:T(128)S(1)}, s32[4]{0:T(128)}, u32[]{:S(2)}) copy-start(s32[4]{0:T(128)} %param.17) | copy-start | bytes 52
  15.1 16.5 %all-to-all-start = ((s32[4,1,1]{2,1,0:T(1,128)}), s32[4,1,1]{2,1,0:T(1,128)S(1)}, u32[]{:S(2)}, u32[]{:S(2)}) async-start(s32[4,1,1]{2,1,0:T(1,128)} %copy.42), calls=%async_computation | async-start | bytes 4096 | tf_op jit(solution)/shard_map/all_to_all | solution.py:48
  31.6 8.8 %all-to-all-start.1 = ((s32[4,1,1]{2,1,0:T(1,128)}), s32[4,1,1]{2,1,0:T(1,128)S(1)}, u32[]{:S(2)}, u32[]{:S(2)}) async-start(s32[4,1,1]{2,1,0:T(1,128)} %copy.43), calls=%async_computation.1 | async-start | bytes 4096 | tf_op jit(solution)/shard_map/all_to_all | solution.py:49
  42.3 8.8 %all-to-all-start.2 = ((bf16[4,16,2048]{2,1,0:T(8,128)(2,1)}), bf16[4,16,2048]{2,1,0:T(8,128)(2,1)S(1)}, u32[]{:S(2)}, u32[]{:S(2)}) async-start(bf16[4,16,2048]{2,1,0:T(8,128)(2,1)} %bitcast.65), calls=%async_computation.3 | async-start | bytes 524288 | tf_op jit(solution)/shard_map/all_to_all | solution.py:47
  56.3 120.7 %copy-start.5 = (bf16[1,2048,768]{2,1,0:T(8,128)(2,1)S(1)}, bf16[1,2048,768]{2,1,0:T(8,128)(2,1)}, u32[]{:S(2)}) copy-start(bf16[1,2048,768]{2,1,0:T(8,128)(2,1)} %param.21) | copy-start | bytes 9437188
  177.0 4.3 %copy-start.6 = (bf16[1,2048,768]{2,1,0:T(8,128)(2,1)S(1)}, bf16[1,2048,768]{2,1,0:T(8,128)(2,1)}, u32[]{:S(2)}) copy-start(bf16[1,2048,768]{2,1,0:T(8,128)(2,1)} %param.22) | copy-start | bytes 9437188
  192.2 5.0 %copy-start.1 = (f32[128,8]{0,1:T(8,128)S(1)}, f32[128,8]{0,1:T(8,128)}, u32[]{:S(2)}) copy-start(f32[128,8]{0,1:T(8,128)} %param.19) | copy-start | bytes 12292
  192.2 132.9 %all-to-all-start.4 = ((bf16[16,80,2048]{2,1,0:T(8,128)(2,1)}), bf16[16,80,2048]{2,1,0:T(8,128)(2,1)}, u32[]{:S(2)}, u32[]{:S(2)}) async-start(bf16[16,80,2048]{2,1,0:T(8,128)(2,1)} %bitcast.61), calls=%async_computation.5 | async-start | bytes 10485760 | tf_op jit(solution)/shard_map/all_to_all | solution.py:78
Sparse Core Ops, SparseCore 0:
  14.5 11.2 reduce-scatter.1
where the time goes:
time: 355 us; the launch traced here: 354 us
  waiting for transfers between devices  137 us (39%)
  blocking collectives  123 us (35%)
  matrix products  33.5 us (9%)
  starting transfers between devices  17.6 us (5%)
  local copies, waits for them, and re-layouts  15.6 us (4%)
  between operations  14.2 us (4%)
  other arithmetic  12.9 us (4%)
    all_to_all x1, waiting for transfers between devices, per_device(): lax.all_to_all(result.reshape(sources, items, width), ('enc', 'exp'), spl...  128 us
    all_to_all x1, blocking collectives, per_device(): lax.all_to_all(outgoing, ('enc', 'exp'), split_axis=0, concat_axis=0, til...  121 us
    gather x1, local copies, waits for them, and re-layouts, per_device(): picked = results[targets].reshape(tok_count, top_count, width)  12 us
  transfers between devices with their start and end apart: 5, of which 3 were waited for; matrix products, arithmetic and copies ran while one was open for 4% of the time, Pallas kernels for 0%

commit v1 on v0

v1 whole, which is shorter than its diff:
```python
import jax
import jax.numpy as jnp
from jax import lax
from jax.sharding import PartitionSpec as P

F32 = jnp.float32
BF16 = jnp.bfloat16


def expert_rows(rows, gate_mat, up_mat, down_mat):
    gate_part = jnp.dot(rows, gate_mat, preferred_element_type=F32)
    up_part = jnp.dot(rows, up_mat, preferred_element_type=F32)
    active = (jax.nn.silu(gate_part) * up_part).astype(BF16)
    return jnp.dot(active, down_mat, preferred_element_type=F32).astype(BF16)


def audio_tokens(tokens, frames, w_patch, w_proj, clip_len, clip_start):
    audio_count = frames.shape[0]
    width = tokens.shape[1]
    tok_count = tokens.shape[0]
    enc_count = lax.axis_size("enc")
    clip_rows = audio_count // enc_count
    grouped = lax.all_gather(frames, "seq", axis=0, tiled=True)
    hidden_cols = jax.nn.gelu(
        jnp.dot(grouped, w_patch, preferred_element_type=F32), approximate=False
    ).astype(BF16)
    embedded = lax.psum_scatter(
        jnp.dot(hidden_cols, w_proj, preferred_element_type=F32),
        "seq",
        scatter_dimension=0,
        tiled=True,
    )
    embedded = embedded.astype(BF16).reshape(enc_count, clip_rows, width)
    arrived = lax.all_to_all(embedded, "enc", split_axis=0, concat_axis=0, tiled=True)
    both = lax.all_to_all(
        jnp.stack([clip_len, clip_start], axis=1), "enc", split_axis=0, concat_axis=0, tiled=True
    )
    lengths, starts = both[:, 0], both[:, 1]
    offsets = jnp.arange(clip_rows, dtype=jnp.int32)
    positions = jnp.where(
        offsets[None, :] < lengths[:, None], starts[:, None] + offsets[None, :], -1
    ).reshape(-1)
    selector = jnp.arange(tok_count, dtype=jnp.int32)[:, None] == positions[None, :]
    placed = jnp.dot(
        selector.astype(BF16), arrived.reshape(-1, width), preferred_element_type=F32
    )
    return jnp.where(jnp.any(selector, axis=1)[:, None], placed.astype(BF16), tokens)


def per_device(
    tokens,
    frames,
    w_patch,
    w_proj,
    clip_len,
    clip_start,
    expert_ids,
    gate_score,
    cotangent,
    w_gate,
    w_up,
    w_down,
):
    width = tokens.shape[1]
    tok_count = tokens.shape[0]
    top_count = expert_ids.shape[1]
    enc_count = lax.axis_size("enc")
    exp_count = lax.axis_size("exp")
    experts = enc_count * exp_count
    capacity = tok_count * top_count * 5 // (4 * experts)
    total = jnp.sum(gate_score, axis=-1, keepdims=True)
    gate = gate_score / total

    expert_axis = jnp.arange(experts, dtype=jnp.int32)[:, None, None]
    chosen = expert_ids.T[None] == expert_axis.transpose(0, 2, 1)
    member = jnp.any(chosen, axis=1)
    earlier = jnp.arange(tok_count)[:, None] < jnp.arange(tok_count)[None, :]
    slot = jnp.dot(member.astype(BF16), earlier.astype(BF16), preferred_element_type=F32)
    slot = jnp.where(member, slot, -1.0)
    weight = jnp.sum(jnp.where(chosen, gate.T[None], 0.0), axis=1)

    me_exp = lax.axis_index("exp")
    info = jnp.stack([slot, weight], axis=0).reshape(2, enc_count, exp_count, tok_count)
    info = info.transpose(2, 0, 1, 3)
    info = lax.all_to_all(info, "exp", split_axis=0, concat_axis=0, tiled=True)
    slot_in, weight_in = info[:, 0], info[:, 1]
    cot_in = lax.all_gather(cotangent, "exp", axis=0)

    mixed = audio_tokens(tokens, frames, w_patch, w_proj, clip_len, clip_start)
    mixed_in = lax.all_gather(mixed, "exp", axis=0)

    place = slot_in[:, :, None, :] == jnp.arange(capacity, dtype=F32)[None, None, :, None]
    outgoing = jnp.einsum(
        "zect,ztd->ezcd", place.astype(BF16), mixed_in, preferred_element_type=F32
    ).astype(BF16)
    received = lax.all_to_all(outgoing, "enc", split_axis=0, concat_axis=0, tiled=True)
    result = expert_rows(
        received.reshape(experts * capacity, width), w_gate[0], w_up[0], w_down[0]
    )
    results = lax.all_to_all(
        result.reshape(enc_count, exp_count, capacity, width),
        "enc",
        split_axis=0,
        concat_axis=0,
        tiled=True,
    )
    spread = jnp.where(place, weight_in[:, :, None, :], 0.0).astype(BF16)
    partial = jnp.einsum("zect,ezcd->ztd", spread, results, preferred_element_type=F32)
    cross = jnp.einsum("ezcd,ztd->zect", results, cot_in, preferred_element_type=F32)
    dots = jnp.sum(jnp.where(place, cross, 0.0), axis=2)
    partial = lax.all_to_all(
        partial.astype(BF16), "exp", split_axis=0, concat_axis=0, tiled=True
    )
    dots = lax.all_to_all(dots, "exp", split_axis=0, concat_axis=0, tiled=True)
    moe_out = jnp.sum(partial.astype(F32), axis=0).astype(BF16)
    dots = dots.transpose(1, 0, 2).reshape(experts, tok_count)
    score_dot = jnp.sum(jnp.where(chosen, dots[:, None, :], 0.0), axis=0).T
    score_grad = (score_dot - jnp.sum(gate * score_dot, axis=-1, keepdims=True)) / total
    return (moe_out, score_grad)


def solution(mesh):
    rows = P(("enc", "seq", "exp"), None)
    line = P(("enc", "seq", "exp"))
    weights = P(("enc", "exp"), None, None)
    in_specs = (
        rows, rows, P(None, "seq"), P("seq", None), line, line, rows, rows, rows,
        weights, weights, weights,
    )
    return jax.shard_map(
        per_device, mesh=mesh, in_specs=in_specs, out_specs=(rows, rows), check_vma=False
    )
```

time: 355 us -> 306 us (0.86)
  the two profiles are of different devices: /device:TPU:0 before, /device:TPU:16 now
where the time goes in v1:
time: 306 us; the launch traced here: 301 us
  waiting for transfers between devices  144 us (47%)
  blocking collectives  81.5 us (27%)
  matrix products  35.8 us (12%)
  starting transfers between devices  18.9 us (6%)
  between operations  13.9 us (5%)
  other arithmetic  5.6 us (2%)
    all_to_all x1, blocking collectives, per_device(): lax.all_to_all(outgoing, 'enc', split_axis=0, concat_axis=0, tiled=True)  62.8 us
    all_gather x1, waiting for transfers between devices, per_device(): cot_in = lax.all_gather(cotangent, 'exp', axis=0)  47.1 us
    all_to_all x1, waiting for transfers between devices, per_device(): lax.all_to_all(partial.astype(BF16), 'exp', split_axis=0, concat_axis=0,...  43.2 us
    all_gather x1, waiting for transfers between devices, per_device(): mixed_in = lax.all_gather(mixed, 'exp', axis=0)  36.1 us
    all_to_all x1, waiting for transfers between devices, per_device(): lax.all_to_all(result.reshape(enc_count, exp_count, capacity, width), 'en...  9.5 us
    all_to_all x1, blocking collectives, per_device(): info = lax.all_to_all(info, 'exp', split_axis=0, concat_axis=0, tiled=True)  8.21 us
    all_to_all x1, blocking collectives, audio_tokens(): lax.all_to_all(jnp.stack([clip_len, clip_start], axis=1), 'enc', split_ax...  8.16 us
  transfers between devices with their start and end apart: 7, of which 6 were waited for; matrix products, arithmetic and copies ran while one was open for 2% of the time, Pallas kernels for 0%

profile of v1, /device:TPU:16, one launch (start us, length us, event | category | flops | bytes accessed | tf_op | source)
XLA Modules:
  0.0 300.7 jit_solution(10342344134896308230)
XLA Ops:
  7.2 2.3 all_gather.15
  9.6 4.7 %fusion.32 = f32[128,2048]{1,0:T(8,128)} fusion(bf16[640,2048]{1,0:T(8,128)(2,1)} %param.15, bf16[128,1024]{1,0:T(8,128)(2,1)S(1)} %all_gather.15, bf16[1024,640]{1,0:T(8,128)(2,1)} %param.14), kind=kOutput, calls=%fused_computation.43 | convolution fusion | flops 508641280 | bytes 5242880 | tf_op jit(solution)/shard_map/dot_general | solution.py:28
  14.3 0.1 copy.35
  14.4 8.2 %all_to_all.42 = s32[4,1,2]{2,1,0:T(1,128)S(1)} all-to-all(s32[4,1,2]{2,1,0:T(1,128)S(1)} %copy.35), channel_id=1, replica_groups=mesh['enc'=4,'seq'=2,'exp'=4] {'enc'}, dimensions={0} | all-to-all | bytes 64 | tf_op jit(solution)/shard_map/all_to_all | solution.py:35
  22.6 0.1 copy.36
  22.7 1.6 reduce-scatter.2.cloned.1.call-done
  24.3 1.8 convert_element_type.35
  26.1 3.6 %all-to-all-start.2 = ((bf16[4,16,2048]{2,1,0:T(8,128)(2,1)}), bf16[4,16,2048]{2,1,0:T(8,128)(2,1)S(1)}, u32[]{:S(2)}, u32[]{:S(2)}) async-start(bf16[4,16,2048]{2,1,0:T(8,128)(2,1)} %bitcast.13), calls=%async_computation.3 | async-start | bytes 524288 | tf_op jit(solution)/shard_map/all_to_all | solution.py:34
  29.8 0.1 select_n.39
  29.9 0.1 fusion.65
  30.0 5.6 %all-to-all-done.2 = bf16[4,16,2048]{2,1,0:T(8,128)(2,1)S(1)} async-done(((bf16[4,16,2048]{2,1,0:T(8,128)(2,1)}), bf16[4,16,2048]{2,1,0:T(8,128)(2,1)S(1)}, u32[]{:S(2)}, u32[]{:S(2)}) %all-to-all-start.2) | async-done | bytes 262176 | tf_op jit(solution)/shard_map/all_to_all | solution.py:34
  35.6 2.2 fusion.11
  38.0 0.1 convolution_select_fusion
  38.1 8.2 %all_to_all.43 = f32[4,2,4,128]{3,2,1,0:T(4,128)S(1)} all-to-all(f32[4,2,4,128]{3,2,1,0:T(4,128)S(1)} %copy.34), channel_id=1, replica_groups=mesh['enc'=4,'seq'=2,'exp'=4] {'exp'}, dimensions={0} | all-to-all | bytes 32768 | tf_op jit(solution)/shard_map/all_to_all | solution.py:85
  46.3 36.1 %all-gather.5.cloned.1.call-done = bf16[512,2048]{1,0:T(8,128)(2,1)} async-done(((bf16[128,2048]{1,0:T(8,128)(2,1)}), bf16[512,2048]{1,0:T(8,128)(2,1)}) %all-gather.5.cloned.1.call-update) | async-done | bytes 2097168 | tf_op jit(solution)/shard_map/all_gather | solution.py:90
  82.4 3.1 %convert_bitcast_fusion = bf16[4,4,80,2048]{3,2,0,1:T(8,128)(2,1)S(1)} fusion(bf16[4,128,2048,1]{2,1,3,0:T(8,128)(2,1)} %bitcast.70, f32[4,4,128]{2,1,0:T(4,128)S(1)} %slice_bitcast_fusion.1), kind=kOutput, calls=%fused_computation.1 | convolution fusion | flops 673873920 | bytes 7348224 | tf_op jit(solution)/shard_map/zect,ztd->ezcd/dot_general | solution.py:93
  85.5 0.8 copy.37
  86.4 62.8 %all_to_all.44 = bf16[4,4,80,2048]{3,2,1,0:T(8,128)(2,1)S(1)} all-to-all(bf16[4,4,80,2048]{3,2,1,0:T(8,128)(2,1)S(1)} %copy.37), channel_id=1, replica_groups=mesh['enc'=4,'seq'=2,'exp'=4] {'enc'}, dimensions={0} | all-to-all | bytes 10485760 | tf_op jit(solution)/shard_map/all_to_all | solution.py:96
  149.2 4.3 %fusion.9 = f32[1280,768]{1,0:T(8,128)S(1)} fusion(bf16[1280,2048]{1,0:T(8,128)(2,1)S(1)} %bitcast.68, bf16[1,2048,768]{2,1,0:T(8,128)(2,1)S(1)} %copy-done.5), kind=kOutput, calls=%fused_computation.11 | convolution fusion | flops 4026531840 | bytes 12320768 | tf_op jit(solution)/shard_map/dot_general | solution.py:11
  153.5 4.8 %fusion.4 = bf16[1280,768]{1,0:T(8,128)(2,1)S(1)} fusion(bf16[1280,2048]{1,0:T(8,128)(2,1)S(1)} %bitcast.69, f32[1280,768]{1,0:T(8,128)S(1)} %fusion.9, bf16[1,2048,768]{2,1,0:T(8,128)(2,1)S(1)} %copy-done.6), kind=kOutput, calls=%fused_computation.8 | convolution fusion | flops 4032430080 | bytes 14286848 | tf_op jit(solution)/shard_map/dot_general | solution.py:12
  158.4 6.1 %convolution_convert_fusion = bf16[1280,2048]{1,0:T(8,128)(2,1)} fusion(bf16[1280,768]{1,0:T(8,128)(2,1)S(1)} %fusion.4, bf16[1,768,2048]{2,1,0:T(8,128)(2,1)S(1)} %copy-done), kind=kOutput, calls=%fused_computation | convolution fusion | flops 4029153280 | bytes 10354688 | tf_op jit(solution)/shard_map/dot_general | solution.py:14
  164.4 5.0 %all-to-all-start.4 = ((bf16[4,4,80,2048]{3,2,1,0:T(8,128)(2,1)}), bf16[4,4,80,2048]{3,2,1,0:T(8,128)(2,1)}, u32[]{:S(2)}, u32[]{:S(2)}) async-start(bf16[4,4,80,2048]{3,2,1,0:T(8,128)(2,1)} %bitcast.67), calls=%async_computation.5 | async-start | bytes 10485760 | tf_op jit(solution)/shard_map/all_to_all | solution.py:100
  169.5 0.7 all-gather.7.cloned.1.call-update
  170.2 47.1 %all-gather.7.cloned.1.call-done = bf16[512,2048]{1,0:T(8,128)(2,1)} async-done(((bf16[128,2048]{1,0:T(8,128)(2,1)}), bf16[512,2048]{1,0:T(8,128)(2,1)}) %all-gather.7.cloned.1.call-update) | async-done | bytes 2097168 | tf_op jit(solution)/shard_map/all_gather | solution.py:87
  217.3 9.5 %all-to-all-done.4 = bf16[4,4,80,2048]{3,2,1,0:T(8,128)(2,1)} async-done(((bf16[4,4,80,2048]{3,2,1,0:T(8,128)(2,1)}), bf16[4,4,80,2048]{3,2,1,0:T(8,128)(2,1)}, u32[]{:S(2)}, u32[]{:S(2)}) %all-to-all-start.4) | async-done | bytes 5242912 | tf_op jit(solution)/shard_map/all_to_all | solution.py:100
  226.8 5.3 %fusion.15 = f32[4,4,128]{2,1,0:T(4,128)} fusion(bf16[4,128,2048,1]{2,1,3,0:T(8,128)(2,1)} %bitcast.82, bf16[4,4,80,2048]{3,2,1,0:T(8,128)(2,1)} %all-to-all-done.4, f32[4,4,128]{2,1,0:T(4,128)S(1)} %slice_bitcast_fusion.1), kind=kOutput, calls=%fused_computation.16 | convolution fusion | flops 671578112 | bytes 7356416 | tf_op jit(solution)/shard_map/ezcd,ztd->zect/dot_general | solution.py:109
  232.1 5.1 %all-to-all-start.6 = ((f32[4,4,128]{2,1,0:T(4,128)}), f32[4,4,128]{2,1,0:T(4,128)S(1)}, u32[]{:S(2)}, u32[]{:S(2)}) async-start(f32[4,4,128]{2,1,0:T(4,128)} %fusion.15), calls=%async_computation.7 | async-start | bytes 16384 | tf_op jit(solution)/shard_map/all_to_all | solution.py:114
  237.2 5.2 %bitcast_convert_fusion = bf16[4,128,2048]{2,1,0:T(8,128)(2,1)} fusion(bf16[4,4,80,2048]{3,2,1,0:T(8,128)(2,1)} %all-to-all-done.4, bf16[4,4,128]{2,1,0:T(4,128)(2,1)S(1)} %slice_bitcast_fusion, f32[4,4,128]{2,1,0:T(4,128)S(1)} %slice_bitcast_fusion.1), kind=kOutput, calls=%fused_computation.6 | convolution fusion | flops 672464896 | bytes 7352320 | tf_op jit(solution)/shard_map/zect,ezcd->ztd/dot_general | solution.py:108
  242.4 5.1 %all-to-all-start.5 = ((bf16[4,128,2048]{2,1,0:T(8,128)(2,1)}), bf16[4,128,2048]{2,1,0:T(8,128)(2,1)}, u32[]{:S(2)}, u32[]{:S(2)}) async-start(bf16[4,128,2048]{2,1,0:T(8,128)(2,1)} %bitcast_convert_fusion), calls=%async_computation.6 | async-start | bytes 4194304 | tf_op jit(solution)/shard_map/all_to_all | solution.py:111
  247.5 0.6 fusion.68
  248.1 43.2 %all-to-all-done.5 = bf16[4,128,2048]{2,1,0:T(8,128)(2,1)} async-done(((bf16[4,128,2048]{2,1,0:T(8,128)(2,1)}), bf16[4,128,2048]{2,1,0:T(8,128)(2,1)}, u32[]{:S(2)}, u32[]{:S(2)}) %all-to-all-start.5) | async-done | bytes 2097184 | tf_op jit(solution)/shard_map/all_to_all | solution.py:111
  291.3 2.9 reduce_sum.59
  (34 shorter events, 0.4 us)
Async XLA Ops:
  7.2 151.2 %copy-start = (bf16[1,768,2048]{2,1,0:T(8,128)(2,1)S(1)}, bf16[1,768,2048]{2,1,0:T(8,128)(2,1)}, u32[]{:S(2)}) copy-start(bf16[1,768,2048]{2,1,0:T(8,128)(2,1)} %param.23) | copy-start | bytes 9437188
  7.2 17.1 %reduce-scatter.2.cloned.1.call-start = ((), (), s32[]{:S(2)}) async-start(), calls=%async_computation.8 | async-start | bytes 1572864 | tf_op jit(solution)/shard_map/reduce_scatter | solution.py:27
  9.6 4.7 %copy-start.3 = (s32[4]{0:T(128)S(1)}, s32[4]{0:T(128)}, u32[]{:S(2)}) copy-start(s32[4]{0:T(128)} %param.17) | copy-start | bytes 52
  9.6 4.7 %copy-start.4 = (s32[4]{0:T(128)S(1)}, s32[4]{0:T(128)}, u32[]{:S(2)}) copy-start(s32[4]{0:T(128)} %param.16) | copy-start | bytes 52
  14.3 23.6 %copy-start.1 = (f32[128,8]{0,1:T(8,128)S(1)}, f32[128,8]{0,1:T(8,128)}, u32[]{:S(2)}) copy-start(f32[128,8]{0,1:T(8,128)} %param.19) | copy-start | bytes 12292
  14.3 23.6 %copy-start.2 = (s32[128,8]{0,1:T(8,128)S(1)}, s32[128,8]{0,1:T(8,128)}, u32[]{:S(2)}) copy-start(s32[128,8]{0,1:T(8,128)} %param.18) | copy-start | bytes 12292
  26.1 9.5 %all-to-all-start.2 = ((bf16[4,16,2048]{2,1,0:T(8,128)(2,1)}), bf16[4,16,2048]{2,1,0:T(8,128)(2,1)S(1)}, u32[]{:S(2)}, u32[]{:S(2)}) async-start(bf16[4,16,2048]{2,1,0:T(8,128)(2,1)} %bitcast.13), calls=%async_computation.3 | async-start | bytes 524288 | tf_op jit(solution)/shard_map/all_to_all | solution.py:34
  29.7 52.7 %all-gather.5.cloned.1.call-start = ((), (), s32[]{:S(2)}) async-start(), calls=%async_computation.9 | async-start | bytes 2621440 | tf_op jit(solution)/shard_map/all_gather | solution.py:90
  86.4 62.8 %copy-start.5 = (bf16[1,2048,768]{2,1,0:T(8,128)(2,1)S(1)}, bf16[1,2048,768]{2,1,0:T(8,128)(2,1)}, u32[]{:S(2)}) copy-start(bf16[1,2048,768]{2,1,0:T(8,128)(2,1)} %param.21) | copy-start | bytes 9437188
  149.2 4.3 %copy-start.6 = (bf16[1,2048,768]{2,1,0:T(8,128)(2,1)S(1)}, bf16[1,2048,768]{2,1,0:T(8,128)(2,1)}, u32[]{:S(2)}) copy-start(bf16[1,2048,768]{2,1,0:T(8,128)(2,1)} %param.22) | copy-start | bytes 9437188
  164.4 62.4 %all-to-all-start.4 = ((bf16[4,4,80,2048]{3,2,1,0:T(8,128)(2,1)}), bf16[4,4,80,2048]{3,2,1,0:T(8,128)(2,1)}, u32[]{:S(2)}, u32[]{:S(2)}) async-start(bf16[4,4,80,2048]{3,2,1,0:T(8,128)(2,1)} %bitcast.67), calls=%async_computation.5 | async-start | bytes 10485760 | tf_op jit(solution)/shard_map/all_to_all | solution.py:100
  169.5 47.9 %all-gather.7.cloned.1.call-start = ((), (), s32[]{:S(2)}) async-start(), calls=%async_computation.10 | async-start | bytes 2621440 | tf_op jit(solution)/shard_map/all_gather | solution.py:87
  232.1 10.3 %all-to-all-start.6 = ((f32[4,4,128]{2,1,0:T(4,128)}), f32[4,4,128]{2,1,0:T(4,128)S(1)}, u32[]{:S(2)}, u32[]{:S(2)}) async-start(f32[4,4,128]{2,1,0:T(4,128)} %fusion.15), calls=%async_computation.7 | async-start | bytes 16384 | tf_op jit(solution)/shard_map/all_to_all | solution.py:114
  242.4 48.9 %all-to-all-start.5 = ((bf16[4,128,2048]{2,1,0:T(8,128)(2,1)}), bf16[4,128,2048]{2,1,0:T(8,128)(2,1)}, u32[]{:S(2)}, u32[]{:S(2)}) async-start(bf16[4,128,2048]{2,1,0:T(8,128)(2,1)} %bitcast_convert_fusion), calls=%async_computation.6 | async-start | bytes 4194304 | tf_op jit(solution)/shard_map/all_to_all | solution.py:111
Sparse Core Ops, SparseCore 0:
  14.4 9.8 reduce-scatter.1
  38.0 44.4 all-gather.4
  171.9 45.3 all-gather.6

commit v2 on v1

--- a/solution.py
+++ b/solution.py
@@ -1,17 +1,250 @@
+import functools
+
 import jax
 import jax.numpy as jnp
 from jax import lax
+from jax.experimental import pallas as pl
+from jax.experimental.pallas import tpu as pltpu
 from jax.sharding import PartitionSpec as P
 
 F32 = jnp.float32
 BF16 = jnp.bfloat16
 
 
-def expert_rows(rows, gate_mat, up_mat, down_mat):
-    gate_part = jnp.dot(rows, gate_mat, preferred_element_type=F32)
-    up_part = jnp.dot(rows, up_mat, preferred_element_type=F32)
-    active = (jax.nn.silu(gate_part) * up_part).astype(BF16)
-    return jnp.dot(active, down_mat, preferred_element_type=F32).astype(BF16)
+MESH = pl.DeviceIdType.MESH
+
+
+def partner(me, step, count, way=1):
+    if count & (count - 1):
+        return lax.rem(me + way * step + count, count)
+    out, bit = 0, 1
+    while bit < count:
+        flip = (step // bit) % 2
+        out = out + ((me // bit + flip) % 2) * bit
+        bit *= 2
+    return out
+
+
+def tile_of(i, size):
+    return pl.ds(pl.multiple_of(i * size, size), size)
+
+
+def exchange_kernel(
+    z_count, e_count, cap,
+    mixed_ref, cot_ref, slot_ref, weight_ref, wg_hbm, wu_hbm, wd_hbm,
+    out_ref, dots_ref,
+    tok, cots, packed, rows, back, part, acc, dot_send, dot_recv, active, wg, wu, wd,
+    w_sem, tok_s, tok_r, cot_s, cot_r, pack_s, pack_r, back_s, back_r, part_s, part_r, dot_s, dot_r,
+):
+    me_z, me_e = lax.axis_index("exp"), lax.axis_index("enc")
+    count, width = mixed_ref.shape
+    hidden = wg.shape[1]
+    items = e_count * cap
+    zs = [partner(me_z, k, z_count) for k in range(z_count)]
+    es = [partner(me_e, j, e_count) for j in range(e_count)]
+    zfrom = [partner(me_z, k, z_count, -1) for k in range(z_count)]
+    efrom = [partner(me_e, j, e_count, -1) for j in range(e_count)]
+
+    loads = [
+        pltpu.make_async_copy(a, b, w_sem.at[i])
+        for i, (a, b) in enumerate(((wg_hbm, wg), (wu_hbm, wu), (wd_hbm, wd)))
+    ]
+    for load in loads:
+        load.start()
+
+    barrier = pltpu.get_barrier_semaphore()
+    for z in zs[1:]:
+        pl.semaphore_signal(barrier, inc=1, device_id={"exp": z}, device_id_type=MESH)
+    for e in es[1:]:
+        pl.semaphore_signal(barrier, inc=1, device_id={"enc": e}, device_id_type=MESH)
+    pl.semaphore_wait(barrier, z_count + e_count - 2)
+
+    def along_z(src, dst, send, recv, k, z):
+        return pltpu.make_async_remote_copy(
+            src_ref=src, dst_ref=dst.at[me_z], send_sem=send.at[k], recv_sem=recv.at[me_z],
+            device_id={"exp": z}, device_id_type=MESH,
+        )
+
+    def landed(dst, recv, c):
+        pltpu.make_async_copy(dst.at[c], dst.at[c], recv.at[c]).wait()
+
+    sent = []
+
+    def go(copy):
+        copy.start()
+        sent.append(copy)
+
+    for k in range(1, z_count):
+        go(along_z(mixed_ref, tok, tok_s, tok_r, k, zs[k]))
+
+    def chosen(c, e):
+        slots = lax.broadcasted_iota(jnp.int32, (cap, count), 0).astype(F32)
+        return slot_ref[c, e] == slots
+
+    def pack(k):
+        c = zfrom[k]
+        if k:
+            landed(tok, tok_r, c)
+        for j in list(range(1, e_count)) + [0]:
+            e = es[j]
+            place = jnp.where(chosen(c, e), 1.0, 0.0).astype(BF16)
+            step = 512
+
+            def body(i, _, place=place, j=j, e=e):
+                cols = tile_of(i, step)
+                source = mixed_ref[:, cols] if k == 0 else tok[c, :, cols]
+                piece = jnp.dot(place, source, preferred_element_type=F32).astype(BF16)
+                if j:
+                    packed[c, e, :, cols] = piece
+                else:
+                    rows[c, e, :, cols] = piece
+                return 0
+
+            lax.fori_loop(0, width // step, body, 0)
+            if j:
+                go(pltpu.make_async_remote_copy(
+                    src_ref=packed.at[c, e], dst_ref=rows.at[c, me_e],
+                    send_sem=pack_s.at[c, e], recv_sem=pack_r.at[c, me_e],
+                    device_id={"enc": e}, device_id_type=MESH,
+                ))
+
+    def work(k):
+        c = zfrom[k]
+        for j in range(1, e_count):
+            e = efrom[j]
+            pltpu.make_async_copy(rows.at[c, e], rows.at[c, e], pack_r.at[c, e]).wait()
+        if k == 0:
+            for load in loads:
+                load.wait()
+
+        def up(i, _):
+            cols = tile_of(i, 256)
+            x = rows[c].reshape(items, width)
+            g = jnp.dot(x, wg[:, cols], preferred_element_type=F32)
+            u = jnp.dot(x, wu[:, cols], preferred_element_type=F32)
+            active[:, cols] = (g / (1.0 + jnp.exp(-g)) * u).astype(BF16)
+            return 0
+
+        lax.fori_loop(0, hidden // 256, up, 0)
+
+        def down(i, _):
+            cols = tile_of(i, 256)
+            y = jnp.dot(active[...], wd[:, cols], preferred_element_type=F32)
+            rows[c, :, :, cols] = y.astype(BF16).reshape(e_count, cap, 256)
+            return 0
+
+        lax.fori_loop(0, width // 256, down, 0)
+        for j in range(1, e_count):
+            e = es[j]
+            go(pltpu.make_async_remote_copy(
+                src_ref=rows.at[c, e], dst_ref=back.at[c, me_e],
+                send_sem=back_s.at[c, e], recv_sem=back_r.at[c, me_e],
+                device_id={"enc": e}, device_id_type=MESH,
+            ))
+        back[c, me_e] = rows[c, me_e]
+
+    def combine(k):
+        c = zfrom[k]
+        for j in range(1, e_count):
+            e = efrom[j]
+            pltpu.make_async_copy(back.at[c, e], back.at[c, e], back_r.at[c, e]).wait()
+        if k:
+            landed(cots, cot_r, c)
+        place = [chosen(c, e) for e in range(e_count)]
+        spread = jnp.concatenate(
+            [jnp.where(place[e], weight_ref[c, e], 0.0) for e in range(e_count)], axis=0
+        ).astype(BF16)
+
+        def total(i, _):
+            cols = tile_of(i, 256)
+            y = back[c, :, :, cols].reshape(items, 256)
+            s = lax.dot_general(spread, y, (((0,), (0,)), ((), ())), preferred_element_type=F32)
+            if k:
+                tok[c, :, cols] = s.astype(BF16)
+            else:
+                acc[:, cols] = s
+            return 0
+
+        lax.fori_loop(0, width // 256, total, 0)
+        if k:
+            go(along_z(tok.at[c], part, part_s, part_r, k, c))
+        other = cot_ref[...] if k == 0 else cots[c]
+        for e in range(e_count):
+            cross = lax.dot_general(
+                back[c, e], other, (((1,), (1,)), ((), ())), preferred_element_type=F32
+            )
+            line = jnp.sum(jnp.where(place[e], cross, 0.0), axis=0, keepdims=True)
+            if k:
+                dot_send[c, e : e + 1, :] = line
+            else:
+                dot_recv[c, e : e + 1, :] = line
+        if k:
+            go(along_z(dot_send.at[c], dot_recv, dot_s, dot_r, k, c))
+
+    for k in range(z_count):
+        pack(k)
+        if k == z_count - 1:
+            for m in range(1, z_count):
+                go(along_z(cot_ref, cots, cot_s, cot_r, m, zs[m]))
+        if k >= 1:
+            work(k - 1)
+        if k >= 3:
+            combine(k - 3)
+    work(z_count - 1)
+    for k in range(max(z_count - 3, 0), z_count):
+        combine(k)
+
+    for k in range(1, z_count):
+        landed(part, part_r, zfrom[k])
+        landed(dot_recv, dot_r, zfrom[k])
+
+    def finish(i, _):
+        cols = tile_of(i, 256)
+        s = acc[:, cols]
+        for k in range(1, z_count):
+            s = s + part[zfrom[k], :, cols].astype(F32)
+        out_ref[:, cols] = s.astype(BF16)
+        return 0
+
+    lax.fori_loop(0, width // 256, finish, 0)
+    dots_ref[...] = dot_recv[...]
+    for copy in sent:
+        copy.wait_send()
+
+
+def exchange(mixed, cot, slot_in, weight_in, w_gate, w_up, w_down, cap):
+    z_count, e_count = slot_in.shape[:2]
+    count, width = mixed.shape
+    hidden = w_gate.shape[1]
+    vmem = pl.BlockSpec(memory_space=pltpu.VMEM)
+    anywhere = pl.BlockSpec(memory_space=pl.ANY)
+    dma = pltpu.SemaphoreType.DMA
+    block = pltpu.VMEM((z_count, e_count, cap, width), BF16)
+    line = pltpu.VMEM((z_count, count, width), BF16)
+    dots = (z_count, e_count, count)
+    return pl.pallas_call(
+        functools.partial(exchange_kernel, z_count, e_count, cap),
+        out_shape=(
+            jax.ShapeDtypeStruct((count, width), BF16),
+            jax.ShapeDtypeStruct(dots, F32),
+        ),
+        in_specs=[vmem] * 4 + [anywhere] * 3,
+        out_specs=(vmem, vmem),
+        scratch_shapes=[
+            line, line, block, block, block, line,
+            pltpu.VMEM((count, width), F32),
+            pltpu.VMEM(dots, F32), pltpu.VMEM(dots, F32),
+            pltpu.VMEM((e_count * cap, hidden), BF16),
+            pltpu.VMEM(w_gate.shape, BF16), pltpu.VMEM(w_up.shape, BF16), pltpu.VMEM(w_down.shape, BF16),
+            dma((3,)), dma((z_count,)), dma((z_count,)), dma((z_count,)), dma((z_count,)),
+            dma((z_count, e_count)), dma((z_count, e_count)),
+            dma((z_count, e_count)), dma((z_count, e_count)),
+            dma((z_count,)), dma((z_count,)), dma((z_count,)), dma((z_count,)),
+        ],
+        compiler_params=pltpu.CompilerParams(
+            collective_id=0, has_side_effects=True, vmem_limit_bytes=60 * 2**20
+        ),
+    )(mixed, cot, slot_in[:, :, None, :], weight_in[:, :, None, :], w_gate, w_up, w_down)
 
 
 def audio_tokens(tokens, frames, w_patch, w_proj, clip_len, clip_start):
@@ -61,7 +294,6 @@
     w_up,
     w_down,
 ):
-    width = tokens.shape[1]
     tok_count = tokens.shape[0]
     top_count = expert_ids.shape[1]
     enc_count = lax.axis_size("enc")
@@ -79,40 +311,15 @@
     slot = jnp.where(member, slot, -1.0)
     weight = jnp.sum(jnp.where(chosen, gate.T[None], 0.0), axis=1)
 
-    me_exp = lax.axis_index("exp")
     info = jnp.stack([slot, weight], axis=0).reshape(2, enc_count, exp_count, tok_count)
     info = info.transpose(2, 0, 1, 3)
     info = lax.all_to_all(info, "exp", split_axis=0, concat_axis=0, tiled=True)
     slot_in, weight_in = info[:, 0], info[:, 1]
-    cot_in = lax.all_gather(cotangent, "exp", axis=0)
-
     mixed = audio_tokens(tokens, frames, w_patch, w_proj, clip_len, clip_start)
-    mixed_in = lax.all_gather(mixed, "exp", axis=0)
-
-    place = slot_in[:, :, None, :] == jnp.arange(capacity, dtype=F32)[None, None, :, None]
-    outgoing = jnp.einsum(
-        "zect,ztd->ezcd", place.astype(BF16), mixed_in, preferred_element_type=F32
-    ).astype(BF16)
-    received = lax.all_to_all(outgoing, "enc", split_axis=0, concat_axis=0, tiled=True)
-    result = expert_rows(
-        received.reshape(experts * capacity, width), w_gate[0], w_up[0], w_down[0]
-    )
-    results = lax.all_to_all(
-        result.reshape(enc_count, exp_count, capacity, width),
-        "enc",
-        split_axis=0,
-        concat_axis=0,
-        tiled=True,
-    )
-    spread = jnp.where(place, weight_in[:, :, None, :], 0.0).astype(BF16)
-    partial = jnp.einsum("zect,ezcd->ztd", spread, results, preferred_element_type=F32)
-    cross = jnp.einsum("ezcd,ztd->zect", results, cot_in, preferred_element_type=F32)
-    dots = jnp.sum(jnp.where(place, cross, 0.0), axis=2)
-    partial = lax.all_to_all(
-        partial.astype(BF16), "exp", split_axis=0, concat_axis=0, tiled=True
-    )
-    dots = lax.all_to_all(dots, "exp", split_axis=0, concat_axis=0, tiled=True)
-    moe_out = jnp.sum(partial.astype(F32), axis=0).astype(BF16)
+    padded = -(-capacity // 16) * 16
+    moe_out, dots = exchange(
+        mixed, cotangent, slot_in, weight_in, w_gate[0], w_up[0], w_down[0], padded
+    )
     dots = dots.transpose(1, 0, 2).reshape(experts, tok_count)
     score_dot = jnp.sum(jnp.where(chosen, dots[:, None, :], 0.0), axis=0).T
     score_grad = (score_dot - jnp.sum(gate * score_dot, axis=-1, keepdims=True)) / total

time: 306 us -> 204 us (0.67); the launches traced: 301 us -> 203 us
  Pallas kernels: 0 us -> 152 us
  waiting for transfers between devices: 144 us -> 9.63 us
  blocking collectives: 81.5 us -> 2.34 us
  matrix products: 35.8 us -> 5.25 us
  starting transfers between devices: 18.9 us -> 12.4 us
  local copies, waits for them, and re-layouts: 1.17 us -> 4.67 us
    pallas_call x0 -> x1, Pallas kernels: none -> 152 us  [exchange(): pl.pallas_call(functools.partial(exchange_kernel, z_count, e_count, cap),...]
    all_gather x2 -> x0, waiting for transfers between devices: 83.2 us -> none  [the longest x1 47.1 us: per_device(): cot_in = lax.all_gather(cotangent, 'exp', axis=0)]
    all_to_all x3 -> x0, blocking collectives: 79.2 us -> none  [the longest x1 62.8 us: per_device(): lax.all_to_all(outgoing, 'enc', split_axis=0, concat_axis=0, tiled=True)]
    all_to_all x3 -> x2, waiting for transfers between devices: 52.7 us -> 4.86 us  [the longest x1 3.72 us: audio_tokens(): lax.all_to_all(jnp.stack([clip_len, clip_start], axis=1), 'enc', split_ax...]
    dot_general x6 -> x0, matrix products: 28.7 us -> none  [the longest x1 6.05 us: expert_rows(): return jnp.dot(active, down_mat, preferred_element_type=F32).astype(BF16)]
    all_to_all x3 -> x2, starting transfers between devices: 15.2 us -> 8.92 us  [the longest x1 5.21 us: per_device(): info = lax.all_to_all(info, 'exp', split_axis=0, concat_axis=0, tiled=True)]
  transfers between devices with their start and end apart: 7 -> 4, of which waited for: 6 -> 3; matrix products, arithmetic and copies ran while one was open for 2% -> 2% of each run, Pallas kernels for 0% -> 0%
where the time goes in v2:
time: 204 us; the launch traced here: 203 us
  Pallas kernels  152 us (75%)
  between operations  14.1 us (7%)
  starting transfers between devices  12.4 us (6%)
  waiting for transfers between devices  9.63 us (5%)
  matrix products  5.25 us (3%)
  local copies, waits for them, and re-layouts  4.67 us (2%)
  other arithmetic  2.68 us (1%)
  blocking collectives  2.34 us (1%)
    pallas_call x1, Pallas kernels, exchange(): pl.pallas_call(functools.partial(exchange_kernel, z_count, e_count, cap),...  152 us
    all_to_all x1, starting transfers between devices, per_device(): info = lax.all_to_all(info, 'exp', split_axis=0, concat_axis=0, tiled=True)  5.21 us
    all_to_all x1, waiting for transfers between devices, audio_tokens(): lax.all_to_all(embedded, 'enc', split_axis=0, concat_axis=0, tiled=True)  4.74 us
  transfers between devices with their start and end apart: 4, of which 3 were waited for; matrix products, arithmetic and copies ran while one was open for 2% of the time, Pallas kernels for 0%

profile of v2, /device:TPU:16, one launch (start us, length us, event | category | flops | bytes accessed | tf_op | source)
XLA Modules:
  0.0 202.7 jit_solution(12773969539831309031)
XLA Ops:
  7.2 0.0 copy-start
  7.2 0.0 reduce-scatter.2.cloned.1.call-start
  7.2 2.3 %all_gather.3 = bf16[128,1024]{1,0:T(8,128)(2,1)S(1)} all-gather(bf16[64,1024]{1,0:T(8,128)(2,1)} %param.13), channel_id=1, replica_groups=mesh['enc'=4,'seq'=2,'exp'=4] {'seq'}, dimensions={0}, use_global_device_ids=true | all-gather | bytes 393216 | tf_op jit(solution)/shard_map/all_gather | solution.py:256
  9.6 0.0 copy-done
  9.6 0.0 copy-start.2
  9.6 0.0 copy-start.3
  9.6 3.9 %fusion.11 = f32[128,2048]{1,0:T(8,128)} fusion(bf16[640,2048]{1,0:T(8,128)(2,1)S(1)} %copy-done, bf16[128,1024]{1,0:T(8,128)(2,1)S(1)} %all_gather.3, bf16[1024,640]{1,0:T(8,128)(2,1)} %param.14), kind=kOutput, calls=%fused_computation.22 | convolution fusion | flops 508641280 | bytes 5242880 | tf_op jit(solution)/shard_map/dot_general | solution.py:261
  13.5 0.0 reduce-scatter.2.cloned.1.call-update
  13.5 0.0 copy-done.4
  13.6 0.7 copy.25
  14.2 3.7 %all-to-all-start = ((s32[4,1,2]{2,1,0:T(1,128)}), s32[4,1,2]{2,1,0:T(1,128)S(1)}, u32[]{:S(2)}, u32[]{:S(2)}) async-start(s32[4,1,2]{2,1,0:T(1,128)} %copy.25), calls=%async_computation | async-start | bytes 4096 | tf_op jit(solution)/shard_map/all_to_all | solution.py:268
  18.0 0.0 copy-done.3
  18.0 0.1 convolution_select_fusion
  18.2 0.6 copy.27
  18.8 3.7 %all-to-all-done = s32[4,1,2]{2,1,0:T(1,128)S(1)} async-done(((s32[4,1,2]{2,1,0:T(1,128)}), s32[4,1,2]{2,1,0:T(1,128)S(1)}, u32[]{:S(2)}, u32[]{:S(2)}) %all-to-all-start) | async-done | bytes 64 | tf_op jit(solution)/shard_map/all_to_all | solution.py:268
  22.5 5.2 %all-to-all-start.2 = ((f32[4,2,4,128]{3,2,1,0:T(4,128)}), f32[4,2,4,128]{3,2,1,0:T(4,128)S(1)}, u32[]{:S(2)}, u32[]{:S(2)}) async-start(f32[4,2,4,128]{3,2,1,0:T(4,128)} %copy.27), calls=%async_computation.3 | async-start | bytes 32768 | tf_op jit(solution)/shard_map/all_to_all | solution.py:316
  27.7 0.1 copy.26
  27.8 0.1 add_select_fusion
  27.9 0.1 select_n.28
  28.0 0.1 fusion.44
  28.1 0.0 reduce-scatter.2.cloned.1.call-done
  28.1 1.8 convert_element_type.13
  29.9 1.1 all-to-all-done.2
  31.0 3.4 %all-to-all-start.1 = ((bf16[4,16,2048]{2,1,0:T(8,128)(2,1)}), bf16[4,16,2048]{2,1,0:T(8,128)(2,1)S(1)}, u32[]{:S(2)}, u32[]{:S(2)}) async-start(bf16[4,16,2048]{2,1,0:T(8,128)(2,1)} %bitcast.6), calls=%async_computation.2 | async-start | bytes 524288 | tf_op jit(solution)/shard_map/all_to_all | solution.py:267
  34.4 0.6 fusion.79
  35.0 4.7 %all-to-all-done.1 = bf16[4,16,2048]{2,1,0:T(8,128)(2,1)S(1)} async-done(((bf16[4,16,2048]{2,1,0:T(8,128)(2,1)}), bf16[4,16,2048]{2,1,0:T(8,128)(2,1)S(1)}, u32[]{:S(2)}, u32[]{:S(2)}) %all-to-all-start.1) | async-done | bytes 262176 | tf_op jit(solution)/shard_map/all_to_all | solution.py:267
  39.8 0.0 copy-done.1
  39.8 1.2 fusion.mixed_ref
  41.0 151.6 %shard_map.131 = (bf16[128,2048]{1,0:T(8,128)(2,1)}, f32[4,4,128]{2,1,0:T(4,128)}) custom-call(bf16[128,2048]{1,0:T(8,128)(2,1)} %fusion.mixed_ref, bf16[128,2048]{1,0:T(8,128)(2,1)} %cot_ref.1, f32[4,4,1,128]{3,2,1,0:T(1,128)} %bitcast.49, f32[4,4,1,128]{3,2,1,0:T(1,128)} %bitcast.48, bf16[2048,768]{1,0:T(8,128)(2,1)} %bitcast.41, ...), custom_call_target="tpu_custom_call" | custom-call | tf_op jit(solution)/shard_map/pallas_call | solution.py:225
  192.6 0.7 copy.30
  193.3 0.6 fusion.47
  193.9 1.9 copy.34
  (14 shorter events, 0.2 us)
Async XLA Ops:
  7.2 2.4 %copy-start = (bf16[640,2048]{1,0:T(8,128)(2,1)S(1)}, bf16[640,2048]{1,0:T(8,128)(2,1)}, u32[]{:S(2)}) copy-start(bf16[640,2048]{1,0:T(8,128)(2,1)} %param.15) | copy-start | bytes 7864324
  7.2 20.9 %reduce-scatter.2.cloned.1.call-start = ((), (), s32[]{:S(2)}) async-start(), calls=%async_computation.4 | async-start | bytes 1572864 | tf_op jit(solution)/shard_map/reduce_scatter | solution.py:260
  9.6 4.0 %copy-start.4 = (s32[4]{0:T(128)S(1)}, s32[4]{0:T(128)}, u32[]{:S(2)}) copy-start(s32[4]{0:T(128)} %param.17) | copy-start | bytes 52
  9.6 4.0 %copy-start.5 = (s32[4]{0:T(128)S(1)}, s32[4]{0:T(128)}, u32[]{:S(2)}) copy-start(s32[4]{0:T(128)} %param.16) | copy-start | bytes 52
  9.6 8.4 %copy-start.2 = (f32[128,8]{0,1:T(8,128)S(1)}, f32[128,8]{0,1:T(8,128)}, u32[]{:S(2)}) copy-start(f32[128,8]{0,1:T(8,128)} %param.19) | copy-start | bytes 12292
  9.6 8.4 %copy-start.3 = (s32[128,8]{0,1:T(8,128)S(1)}, s32[128,8]{0,1:T(8,128)}, u32[]{:S(2)}) copy-start(s32[128,8]{0,1:T(8,128)} %param.18) | copy-start | bytes 12292
  13.5 26.3 %copy-start.1 = (bf16[128,2048]{1,0:T(8,128)(2,1)S(1)}, bf16[128,2048]{1,0:T(8,128)(2,1)}, u32[]{:S(2)}) copy-start(bf16[128,2048]{1,0:T(8,128)(2,1)} %param.12) | copy-start | bytes 1572868
  14.2 8.3 %all-to-all-start = ((s32[4,1,2]{2,1,0:T(1,128)}), s32[4,1,2]{2,1,0:T(1,128)S(1)}, u32[]{:S(2)}, u32[]{:S(2)}) async-start(s32[4,1,2]{2,1,0:T(1,128)} %copy.25), calls=%async_computation | async-start | bytes 4096 | tf_op jit(solution)/shard_map/all_to_all | solution.py:268
  22.5 8.5 %all-to-all-start.2 = ((f32[4,2,4,128]{3,2,1,0:T(4,128)}), f32[4,2,4,128]{3,2,1,0:T(4,128)S(1)}, u32[]{:S(2)}, u32[]{:S(2)}) async-start(f32[4,2,4,128]{3,2,1,0:T(4,128)} %copy.27), calls=%async_computation.3 | async-start | bytes 32768 | tf_op jit(solution)/shard_map/all_to_all | solution.py:316
  31.0 8.8 %all-to-all-start.1 = ((bf16[4,16,2048]{2,1,0:T(8,128)(2,1)}), bf16[4,16,2048]{2,1,0:T(8,128)(2,1)S(1)}, u32[]{:S(2)}, u32[]{:S(2)}) async-start(bf16[4,16,2048]{2,1,0:T(8,128)(2,1)} %bitcast.6), calls=%async_computation.2 | async-start | bytes 524288 | tf_op jit(solution)/shard_map/all_to_all | solution.py:267
Sparse Core Ops, SparseCore 0:
  13.7 9.8 reduce-scatter.1

commit v3 on v2

--- a/solution.py
+++ b/solution.py
@@ -30,26 +30,34 @@
 
 
 def exchange_kernel(
-    z_count, e_count, cap,
-    mixed_ref, cot_ref, slot_ref, weight_ref, wg_hbm, wu_hbm, wd_hbm,
+    z_count, e_count, s_count, cap, clip_rows,
+    tok_ref, frames_ref, pos_ref, info_ref, cot_ref, wa_hbm, wb_hbm, wg_hbm, wu_hbm, wd_hbm,
     out_ref, dots_ref,
-    tok, cots, packed, rows, back, part, acc, dot_send, dot_recv, active, wg, wu, wd,
+    tok, cots, packed, rows, back, part, dot_send, dot_recv, active, wg, wu, wd,
+    mixed_ref, wa, heard, grouped, share, shares, embedded, arrived, pos, info,
     w_sem, tok_s, tok_r, cot_s, cot_r, pack_s, pack_r, back_s, back_r, part_s, part_r, dot_s, dot_r,
+    frame_s, frame_r, share_s, share_r, clip_s, clip_r, pos_s, pos_r, info_s, info_r,
 ):
-    me_z, me_e = lax.axis_index("exp"), lax.axis_index("enc")
+    me_z, me_e, me_s = lax.axis_index("exp"), lax.axis_index("enc"), lax.axis_index("seq")
     count, width = mixed_ref.shape
     hidden = wg.shape[1]
     items = e_count * cap
     zs = [partner(me_z, k, z_count) for k in range(z_count)]
     es = [partner(me_e, j, e_count) for j in range(e_count)]
     zfrom = [partner(me_z, k, z_count, -1) for k in range(z_count)]
+    ss = [partner(me_s, j, s_count) for j in range(s_count)]
+    sfrom = [partner(me_s, j, s_count, -1) for j in range(s_count)]
     efrom = [partner(me_e, j, e_count, -1) for j in range(e_count)]
 
+    units = wb_hbm.shape[0]
+    wb = wd.at[pl.ds(0, units)]
     loads = [
         pltpu.make_async_copy(a, b, w_sem.at[i])
-        for i, (a, b) in enumerate(((wg_hbm, wg), (wu_hbm, wu), (wd_hbm, wd)))
+        for i, (a, b) in enumerate(
+            ((wa_hbm, wa), (wb_hbm, wb), (wg_hbm, wg), (wu_hbm, wu), (wd_hbm, wd))
+        )
     ]
-    for load in loads:
+    for load in loads[:4]:
         load.start()
 
     barrier = pltpu.get_barrier_semaphore()
@@ -57,7 +65,9 @@
         pl.semaphore_signal(barrier, inc=1, device_id={"exp": z}, device_id_type=MESH)
     for e in es[1:]:
         pl.semaphore_signal(barrier, inc=1, device_id={"enc": e}, device_id_type=MESH)
-    pl.semaphore_wait(barrier, z_count + e_count - 2)
+    for q in ss[1:]:
+        pl.semaphore_signal(barrier, inc=1, device_id={"seq": q}, device_id_type=MESH)
+    pl.semaphore_wait(barrier, z_count + e_count + s_count - 3)
 
     def along_z(src, dst, send, recv, k, z):
         return pltpu.make_async_remote_copy(
@@ -74,12 +84,92 @@
         copy.start()
         sent.append(copy)
 
+    def across(axis, me, src, dst, send, recv, j, to):
+        return pltpu.make_async_remote_copy(
+            src_ref=src, dst_ref=dst.at[me], send_sem=send.at[j], recv_sem=recv.at[me],
+            device_id={axis: to}, device_id_type=MESH,
+        )
+
+    for j in range(1, s_count):
+        go(across("seq", me_s, frames_ref, grouped, frame_s, frame_r, j, ss[j]))
+    for j in range(1, e_count):
+        go(across("enc", me_e, pos_ref.at[es[j]], pos, pos_s, pos_r, j, es[j]))
+    for k in range(1, z_count):
+        go(along_z(info_ref.at[zs[k]], info, info_s, info_r, k, zs[k]))
+    early = max(z_count // 2, 1)
+    for k in range(1, early + 1):
+        if k < z_count:
+            go(along_z(cot_ref, cots, cot_s, cot_r, k, zs[k]))
+    grouped[me_s] = frames_ref[...]
+    pos[me_e] = pos_ref[me_e]
+    info[me_z] = info_ref[me_z]
+    loads[0].wait()
+    for j in range(1, s_count):
+        landed(grouped, frame_r, sfrom[j])
+    audio = frames_ref.shape[0]
+    lines = jnp.dot(
+        grouped[...].reshape(s_count * audio, frames_ref.shape[1]), wa[...],
+        preferred_element_type=F32,
+    )
+    lines = (0.5 * lines * (1.0 + lax.erf(lines * (0.5**0.5)))).astype(BF16)
+    loads[1].wait()
+    heard[...] = lines
+
+    def project(i, _):
+        cols = tile_of(i, 256)
+        y = jnp.dot(heard[...], wd[:units, cols], preferred_element_type=F32)
+        share[:, :, cols] = y.reshape(s_count, audio, 256)
+        return 0
+
+    lax.fori_loop(0, width // 256, project, 0)
+    loads[4].start()
+    for j in range(1, s_count):
+        go(across("seq", me_s, share.at[ss[j]], shares, share_s, share_r, j, ss[j]))
+    for j in range(1, s_count):
+        landed(shares, share_r, sfrom[j])
+
+    def add(i, _):
+        cols = tile_of(i, 256)
+        y = share[me_s, :, cols]
+        for j in range(1, s_count):
+            y = y + shares[sfrom[j], :, cols]
+        embedded[:, :, cols] = y.astype(BF16).reshape(e_count, clip_rows, 256)
+        return 0
+
+    lax.fori_loop(0, width // 256, add, 0)
+    for j in range(1, e_count):
+        go(across("enc", me_e, embedded.at[es[j]], arrived, clip_s, clip_r, j, es[j]))
+    arrived[me_e] = embedded[me_e]
+    for j in range(1, e_count):
+        landed(pos, pos_r, efrom[j])
+    at = jnp.full((1, pos.shape[2]), -1.0, F32)
+    for e in range(e_count):
+        at = jnp.maximum(at, pos[e])
+    line = lax.broadcasted_iota(jnp.int32, (count, pos.shape[2]), 0).astype(F32)
+    picked = jnp.where(at == line, 1.0, 0.0)
+    taken = jnp.sum(picked, axis=1, keepdims=True)
+    picked = picked[:, : e_count * clip_rows].astype(BF16)
+    for j in range(1, e_count):
+        landed(arrived, clip_r, efrom[j])
+
+    def mix(i, _):
+        cols = tile_of(i, 256)
+        y = arrived[:, :, cols].reshape(e_count * clip_rows, 256)
+        y = jnp.dot(picked, y, preferred_element_type=F32)
+        keep = tok_ref[:, cols].astype(F32)
+        mixed_ref[:, cols] = jnp.where(taken > 0.0, y, keep).astype(BF16)
+        return 0
+
+    lax.fori_loop(0, width // 256, mix, 0)
+
     for k in range(1, z_count):
         go(along_z(mixed_ref, tok, tok_s, tok_r, k, zs[k]))
+    for k in range(1, z_count):
+        landed(info, info_r, zfrom[k])
 
     def chosen(c, e):
         slots = lax.broadcasted_iota(jnp.int32, (cap, count), 0).astype(F32)
-        return slot_ref[c, e] == slots
+        return info[c, e] == slots
 
     def pack(k):
         c = zfrom[k]
@@ -114,7 +204,7 @@
             e = efrom[j]
             pltpu.make_async_copy(rows.at[c, e], rows.at[c, e], pack_r.at[c, e]).wait()
         if k == 0:
-            for load in loads:
+            for load in loads[2:]:
                 load.wait()
 
         def up(i, _):
@@ -152,7 +242,7 @@
             landed(cots, cot_r, c)
         place = [chosen(c, e) for e in range(e_count)]
         spread = jnp.concatenate(
-            [jnp.where(place[e], weight_ref[c, e], 0.0) for e in range(e_count)], axis=0
+            [jnp.where(place[e], info[c, e_count + e], 0.0) for e in range(e_count)], axis=0
         ).astype(BF16)
 
         def total(i, _):
@@ -162,7 +252,7 @@
             if k:
                 tok[c, :, cols] = s.astype(BF16)
             else:
-                acc[:, cols] = s
+                shares[:, : count // s_count, cols] = s.reshape(s_count, count // s_count, 256)
             return 0
 
         lax.fori_loop(0, width // 256, total, 0)
@@ -184,7 +274,7 @@
     for k in range(z_count):
         pack(k)
         if k == z_count - 1:
-            for m in range(1, z_count):
+            for m in range(early + 1, z_count):
                 go(along_z(cot_ref, cots, cot_s, cot_r, m, zs[m]))
         if k >= 1:
             work(k - 1)
@@ -200,7 +290,7 @@
 
     def finish(i, _):
         cols = tile_of(i, 256)
-        s = acc[:, cols]
+        s = shares[:, : count // s_count, cols].reshape(count, 256)
         for k in range(1, z_count):
             s = s + part[zfrom[k], :, cols].astype(F32)
         out_ref[:, cols] = s.astype(BF16)
@@ -212,9 +302,12 @@
         copy.wait_send()
 
 
-def exchange(mixed, cot, slot_in, weight_in, w_gate, w_up, w_down, cap):
-    z_count, e_count = slot_in.shape[:2]
-    count, width = mixed.shape
+def exchange(tokens, frames, pos, info, cot, w_patch, w_proj, w_gate, w_up, w_down, cap):
+    z_count, e_count, s_count = (lax.axis_size(a) for a in ("exp", "enc", "seq"))
+    count, width = tokens.shape
+    audio = frames.shape[0]
+    units = w_patch.shape[1]
+    clip_rows = audio // e_count
     hidden = w_gate.shape[1]
     vmem = pl.BlockSpec(memory_space=pltpu.VMEM)
     anywhere = pl.BlockSpec(memory_space=pl.ANY)
@@ -223,61 +316,45 @@
     line = pltpu.VMEM((z_count, count, width), BF16)
     dots = (z_count, e_count, count)
     return pl.pallas_call(
-        functools.partial(exchange_kernel, z_count, e_count, cap),
+        functools.partial(exchange_kernel, z_count, e_count, s_count, cap, clip_rows),
         out_shape=(
             jax.ShapeDtypeStruct((count, width), BF16),
             jax.ShapeDtypeStruct(dots, F32),
         ),
-        in_specs=[vmem] * 4 + [anywhere] * 3,
+        in_specs=[vmem] * 5 + [anywhere] * 5,
         out_specs=(vmem, vmem),
         scratch_shapes=[
             line, line, block, block, block, line,
-            pltpu.VMEM((count, width), F32),
             pltpu.VMEM(dots, F32), pltpu.VMEM(dots, F32),
             pltpu.VMEM((e_count * cap, hidden), BF16),
             pltpu.VMEM(w_gate.shape, BF16), pltpu.VMEM(w_up.shape, BF16), pltpu.VMEM(w_down.shape, BF16),
-            dma((3,)), dma((z_count,)), dma((z_count,)), dma((z_count,)), dma((z_count,)),
+            pltpu.VMEM((count, width), BF16),
+            pltpu.VMEM(w_patch.shape, BF16),
+            pltpu.VMEM((s_count * audio, units), BF16),
+            pltpu.VMEM((s_count,) + frames.shape, BF16),
+            pltpu.VMEM((s_count, audio, width), F32), pltpu.VMEM((s_count, audio, width), F32),
+            pltpu.VMEM((e_count, clip_rows, width), BF16), pltpu.VMEM((e_count, clip_rows, width), BF16),
+            pltpu.VMEM(pos.shape, F32), pltpu.VMEM(info.shape, F32),
+            dma((5,)), dma((z_count,)), dma((z_count,)), dma((z_count,)), dma((z_count,)),
             dma((z_count, e_count)), dma((z_count, e_count)),
             dma((z_count, e_count)), dma((z_count, e_count)),
             dma((z_count,)), dma((z_count,)), dma((z_count,)), dma((z_count,)),
+            dma((s_count,)), dma((s_count,)), dma((s_count,)), dma((s_count,)),
+            dma((e_count,)), dma((e_count,)), dma((e_count,)), dma((e_count,)),
+            dma((z_count,)), dma((z_count,)),
         ],
         compiler_params=pltpu.CompilerParams(
             collective_id=0, has_side_effects=True, vmem_limit_bytes=60 * 2**20
         ),
-    )(mixed, cot, slot_in[:, :, None, :], weight_in[:, :, None, :], w_gate, w_up, w_down)
-
-
-def audio_tokens(tokens, frames, w_patch, w_proj, clip_len, clip_start):
-    audio_count = frames.shape[0]
-    width = tokens.shape[1]
-    tok_count = tokens.shape[0]
-    enc_count = lax.axis_size("enc")
-    clip_rows = audio_count // enc_count
-    grouped = lax.all_gather(frames, "seq", axis=0, tiled=True)
-    hidden_cols = jax.nn.gelu(
-        jnp.dot(grouped, w_patch, preferred_element_type=F32), approximate=False
-    ).astype(BF16)
-    embedded = lax.psum_scatter(
-        jnp.dot(hidden_cols, w_proj, preferred_element_type=F32),
-        "seq",
-        scatter_dimension=0,
-        tiled=True,
-    )
-    embedded = embedded.astype(BF16).reshape(enc_count, clip_rows, width)
-    arrived = lax.all_to_all(embedded, "enc", split_axis=0, concat_axis=0, tiled=True)
-    both = lax.all_to_all(
-        jnp.stack([clip_len, clip_start], axis=1), "enc", split_axis=0, concat_axis=0, tiled=True
-    )
-    lengths, starts = both[:, 0], both[:, 1]
-    offsets = jnp.arange(clip_rows, dtype=jnp.int32)
-    positions = jnp.where(
-        offsets[None, :] < lengths[:, None], starts[:, None] + offsets[None, :], -1
-    ).reshape(-1)
-    selector = jnp.arange(tok_count, dtype=jnp.int32)[:, None] == positions[None, :]
-    placed = jnp.dot(
-        selector.astype(BF16), arrived.reshape(-1, width), preferred_element_type=F32
-    )
-    return jnp.where(jnp.any(selector, axis=1)[:, None], placed.astype(BF16), tokens)
+    )(tokens, frames, pos, info, cot, w_patch, w_proj, w_gate, w_up, w_down)
+
+
+def positions(clip_len, clip_start, clip_rows):
+    e_count = clip_len.shape[0]
+    lanes = -(-e_count * clip_rows // 128) * 128
+    lane = jnp.arange(lanes, dtype=jnp.int32) - lax.axis_index("enc") * clip_rows
+    mine = (lane[None, :] >= 0) & (lane[None, :] < clip_len[:, None])
+    return jnp.where(mine, clip_start[:, None] + lane[None, :], -1).astype(F32)[:, None, :]
 
 
 def per_device(
@@ -311,14 +388,12 @@
     slot = jnp.where(member, slot, -1.0)
     weight = jnp.sum(jnp.where(chosen, gate.T[None], 0.0), axis=1)
 
-    info = jnp.stack([slot, weight], axis=0).reshape(2, enc_count, exp_count, tok_count)
-    info = info.transpose(2, 0, 1, 3)
-    info = lax.all_to_all(info, "exp", split_axis=0, concat_axis=0, tiled=True)
-    slot_in, weight_in = info[:, 0], info[:, 1]
-    mixed = audio_tokens(tokens, frames, w_patch, w_proj, clip_len, clip_start)
+    info = jnp.stack([slot, weight], axis=0).reshape(2, enc_count, exp_count, 1, tok_count)
+    info = info.transpose(2, 0, 1, 3, 4).reshape(exp_count, 2 * enc_count, 1, tok_count)
+    pos = positions(clip_len, clip_start, frames.shape[0] // enc_count)
     padded = -(-capacity // 16) * 16
     moe_out, dots = exchange(
-        mixed, cotangent, slot_in, weight_in, w_gate[0], w_up[0], w_down[0], padded
+        tokens, frames, pos, info, cotangent, w_patch, w_proj, w_gate[0], w_up[0], w_down[0], padded
     )
     dots = dots.transpose(1, 0, 2).reshape(experts, tok_count)
     score_dot = jnp.sum(jnp.where(chosen, dots[:, None, :], 0.0), axis=0).T

time: 204 us -> 187 us (0.917)
  Pallas kernels: 152 us -> 178 us
  between operations: 14.1 us -> 0.65 us
  starting transfers between devices: 12.4 us -> 0 us
  waiting for transfers between devices: 9.63 us -> 0 us
  matrix products: 5.25 us -> 0.14 us
  blocking collectives: 2.34 us -> 0 us
  other arithmetic: 2.68 us -> 4.82 us
    pallas_call x1, Pallas kernels: 152 us -> 178 us  [exchange(): pl.pallas_call(functools.partial(exchange_kernel, z_count, e_count, s_cou...]
    all_to_all x3 -> x0, starting transfers between devices: 12.3 us -> none  [the longest x1 5.21 us: per_device(): info = lax.all_to_all(info, 'exp', split_axis=0, concat_axis=0, tiled=True)]
    all_to_all x3 -> x0, waiting for transfers between devices: 9.59 us -> none  [the longest x1 4.74 us: audio_tokens(): lax.all_to_all(embedded, 'enc', split_axis=0, concat_axis=0, tiled=True)]
    dot_general x2 -> x0, matrix products: 5.12 us -> none  [the longest x1 3.91 us: audio_tokens(): jnp.dot(hidden_cols, w_proj, preferred_element_type=F32)]
    all_gather x1 -> x0, blocking collectives: 2.34 us -> none  [audio_tokens(): grouped = lax.all_gather(frames, 'seq', axis=0, tiled=True)]
  transfers between devices with their start and end apart: 4 -> 0, of which waited for: 3 -> 0; matrix products, arithmetic and copies ran while one was open for 2% -> 0% of each run, Pallas kernels for 0% -> 0%
where the time goes in v3:
time: 187 us
  Pallas kernels  178 us (95%)
  other arithmetic  4.82 us (3%)
  local copies, waits for them, and re-layouts  3.21 us (2%)
    pallas_call x1, Pallas kernels, exchange(): pl.pallas_call(functools.partial(exchange_kernel, z_count, e_count, s_cou...  178 us

profile of v3, /device:TPU:16, one launch (start us, length us, event | category | flops | bytes accessed | tf_op | source)
XLA Modules:
  0.0 186.6 jit_solution(7802704648205801239)
XLA Ops:
  0.6 0.7 reduce_sum.36
  1.3 0.7 fusion.4
  2.0 0.7 select_reduce_fusion.1
  2.7 0.7 fusion
  3.5 0.1 convolution_select_fusion
  3.6 0.6 copy.17
  4.2 1.3 fusion.3.pos_ref
  5.6 0.0 copy-start.1
  5.6 0.0 copy-start
  5.6 177.8 %shard_map.131 = (bf16[128,2048]{1,0:T(8,128)(2,1)}, f32[4,4,128]{2,1,0:T(4,128)}) custom-call(bf16[128,2048]{1,0:T(8,128)(2,1)} %tok_ref.1, bf16[64,1024]{1,0:T(8,128)(2,1)} %frames_ref.1, f32[4,1,128]{2,1,0:T(1,128)} %fusion.3.pos_ref, f32[4,8,1,128]{3,2,1,0:T(1,128)} %bitcast.24, bf16[128,2048]{1,0:T(8,128)(2,1)} %cot_ref.1, bf16[1024,640]{1,0:T(8,128)(2,1)} %wa_hbm.1, ...), custom_call_target="tpu_custom_call" | custom-call | tf_op jit(solution)/shard_map/pallas_call | solution.py:318
  183.4 0.7 copy.18
  184.1 0.0 copy-done.1
  184.1 0.0 copy-done
  184.1 0.6 fusion.2
  184.7 1.9 %copy.20 = bf16[128,2048]{1,0:T(8,128)(2,1)} copy(bf16[128,2048]{1,0:T(8,128)(2,1)} %get-tuple-element.8) | data formatting | bytes 1048576
  (5 shorter events, 0.1 us)
Async XLA Ops:
  5.6 178.5 %copy-start.1 = (s32[128,8]{0,1:T(8,128)S(1)}, s32[128,8]{0,1:T(8,128)}, u32[]{:S(2)}) copy-start(s32[128,8]{0,1:T(8,128)} %param.18) | copy-start | bytes 12292
  5.6 178.5 %copy-start = (f32[128,8]{0,1:T(8,128)S(1)}, f32[128,8]{0,1:T(8,128)}, u32[]{:S(2)}) copy-start(f32[128,8]{0,1:T(8,128)} %param.19) | copy-start | bytes 12292

commit v4 on v3

--- a/solution.py
+++ b/solution.py
@@ -162,7 +162,8 @@
 
     lax.fori_loop(0, width // 256, mix, 0)
 
-    for k in range(1, z_count):
+    order = [0] + list(range(2, z_count)) + [1]
+    for k in order[1:]:
         go(along_z(mixed_ref, tok, tok_s, tok_r, k, zs[k]))
     for k in range(1, z_count):
         landed(info, info_r, zfrom[k])
@@ -271,18 +272,18 @@
         if k:
             go(along_z(dot_send.at[c], dot_recv, dot_s, dot_r, k, c))
 
-    for k in range(z_count):
+    for k in order[:2]:
         pack(k)
-        if k == z_count - 1:
-            for m in range(early + 1, z_count):
-                go(along_z(cot_ref, cots, cot_s, cot_r, m, zs[m]))
-        if k >= 1:
-            work(k - 1)
-        if k >= 3:
-            combine(k - 3)
-    work(z_count - 1)
-    for k in range(max(z_count - 3, 0), z_count):
-        combine(k)
+        work(k)
+    for k in order[2:]:
+        pack(k)
+    for m in range(early + 1, z_count):
+        go(along_z(cot_ref, cots, cot_s, cot_r, m, zs[m]))
+    combine(order[0])
+    for last, k in zip(order[1:], order[2:]):
+        work(k)
+        combine(last)
+    combine(order[-1])
 
     for k in range(1, z_count):
         landed(part, part_r, zfrom[k])

time: 187 us -> 179 us (0.957)
  Pallas kernels: 178 us -> 169 us
    pallas_call x1, Pallas kernels: 178 us -> 169 us  [exchange(): pl.pallas_call(functools.partial(exchange_kernel, z_count, e_count, s_cou...]
where the time goes in v4:
time: 179 us; the launch traced here: 178 us
  Pallas kernels  169 us (94%)
  other arithmetic  4.82 us (3%)
  local copies, waits for them, and re-layouts  3.21 us (2%)
    pallas_call x1, Pallas kernels, exchange(): pl.pallas_call(functools.partial(exchange_kernel, z_count, e_count, s_cou...  169 us

profile of v4, /device:TPU:16, one launch (start us, length us, event | category | flops | bytes accessed | tf_op | source)
XLA Modules:
  0.0 178.1 jit_solution(657208853617458530)
XLA Ops:
  0.6 0.7 reduce_sum.36
  1.3 0.7 fusion.4
  2.0 0.7 select_reduce_fusion.1
  2.7 0.7 fusion
  3.5 0.1 convolution_select_fusion
  3.6 0.6 copy.17
  4.2 1.3 fusion.3.pos_ref
  5.6 0.0 copy-start.1
  5.6 0.0 copy-start
  5.6 169.3 %shard_map.131 = (bf16[128,2048]{1,0:T(8,128)(2,1)}, f32[4,4,128]{2,1,0:T(4,128)}) custom-call(bf16[128,2048]{1,0:T(8,128)(2,1)} %tok_ref.1, bf16[64,1024]{1,0:T(8,128)(2,1)} %frames_ref.1, f32[4,1,128]{2,1,0:T(1,128)} %fusion.3.pos_ref, f32[4,8,1,128]{3,2,1,0:T(1,128)} %bitcast.24, bf16[128,2048]{1,0:T(8,128)(2,1)} %cot_ref.1, bf16[1024,640]{1,0:T(8,128)(2,1)} %wa_hbm.1, ...), custom_call_target="tpu_custom_call" | custom-call | tf_op jit(solution)/shard_map/pallas_call | solution.py:319
  174.9 0.7 copy.18
  175.6 0.0 copy-done.1
  175.6 0.0 copy-done
  175.7 0.6 fusion.2
  176.3 1.9 %copy.20 = bf16[128,2048]{1,0:T(8,128)(2,1)} copy(bf16[128,2048]{1,0:T(8,128)(2,1)} %get-tuple-element.8) | data formatting | bytes 1048576
  (5 shorter events, 0.1 us)
Async XLA Ops:
  5.6 170.0 %copy-start.1 = (s32[128,8]{0,1:T(8,128)S(1)}, s32[128,8]{0,1:T(8,128)}, u32[]{:S(2)}) copy-start(s32[128,8]{0,1:T(8,128)} %param.18) | copy-start | bytes 12292
  5.6 170.1 %copy-start = (f32[128,8]{0,1:T(8,128)S(1)}, f32[128,8]{0,1:T(8,128)}, u32[]{:S(2)}) copy-start(f32[128,8]{0,1:T(8,128)} %param.19) | copy-start | bytes 12292
